TPU v7x, 256 devices: a whole 4x4x8 slice. The times are simulated.
256 devices in a mesh: rep: 32 (over z, x_hi, core), tp: 8 (over x_lo, y).
Axes of the slice: x: 4 (x_hi: 2, x_lo: 2; x = x_hi * 2 + x_lo), y: 4, z: 8, core: 2. Of those that a mesh axis runs over, the one named last changes fastest.
Arguments:
- inputs: bfloat16 [6144, 2560], P(('rep', 'tp')), may hold values from -6 to 6
- cotangent: bfloat16 [6144, 2560], P(('rep', 'tp')), may hold values from -6 to 6
- gate_weight: bfloat16 [32, 2560, 2048], P('rep', None, 'tp'), may hold values from -0.125 to 0.125
- up_weight: bfloat16 [32, 2560, 2048], P('rep', None, 'tp'), may hold values from -0.125 to 0.125
- down_weight: bfloat16 [32, 2048, 2560], P('rep', 'tp'), may hold values from -0.0625 to 0.0625
- gate_moment: bfloat16 [32, 2560, 2048], P('rep', None, 'tp'), may hold values from -48 to 48
- up_moment: bfloat16 [32, 2560, 2048], P('rep', None, 'tp'), may hold values from -48 to 48
- down_moment: bfloat16 [32, 2048, 2560], P('rep', 'tp'), may hold values from -48 to 48
- step_count: int32 [], replicated, may hold values from 0 to 999
Outputs:
- block_out: bfloat16 [6144, 2560], P(('rep', 'tp'))
- input_grad: bfloat16 [6144, 2560], P(('rep', 'tp'))
- new_gate: bfloat16 [32, 2560, 2048], P('rep', None, 'tp')
- new_up: bfloat16 [32, 2560, 2048], P('rep', None, 'tp')
- new_down: bfloat16 [32, 2048, 2560], P('rep', 'tp')
All inputs are finite; a program needn't handle non-finite values.
Results may differ from a plain program's by a relative error of at most 0.0058.
Values may be sent and summed in bfloat16 or wider, within the bound.
A program may use at most 128 MiB of HBM per device.

v0:
```python
import functools

import jax
import jax.numpy as jnp
from jax import lax
from jax.experimental import pallas as pl
from jax.experimental.pallas import tpu as pltpu
from jax.sharding import PartitionSpec as P

MESH = pl.DeviceIdType.MESH
SPLIT = 4
SIDE = 4
MOMENT = 0.9
LEARN = 0.001
CHUNK = 512
FLAGS = ()
EARLY = (192, 80, 80)
F32 = jnp.float32
BF16 = jnp.bfloat16


def at_multiple(index, of):
    return pl.multiple_of(index, of)


def kernel(
    level,
    x_in,
    g_in,
    wg_in,
    wu_in,
    wd_in,
    mg_in,
    mu_in,
    md_in,
    out_o,
    gin_o,
    ng_o,
    nu_o,
    nd_o,
    x3,
    g3,
    xc,
    gc,
    wg,
    wu,
    wd,
    mg,
    mu,
    md,
    rg,
    ru,
    rd,
    gate,
    up,
    act,
    gb,
    ub,
    actt,
    he,
    gp3,
    actp,
    sx,
    sg,
    px,
    pg,
    load_sem,
    own_sem,
    wave_send,
    wave_recv,
    pair_send,
    pair_recv,
    sum_send,
    sum_recv,
    gossip_send,
    gossip_recv,
    write_sem,
):
    rows, depth = x_in.shape
    width = wg.shape[1]
    blocks = SIDE * SIDE
    half = blocks * rows
    r, t = lax.axis_index("rep"), lax.axis_index("tp")
    z, core = r // SPLIT, r % 2
    x, y = (r // 2) % 2 * 2 + t // SIDE, t % SIDE
    s = x + core * (y - x)
    f = y + core * (x - y)

    def turn(index):
        return (index + SIDE) % SIDE

    def device(cc, ss, ff, zz=None):
        xx = ss + cc * (ff - ss)
        yy = ff + cc * (ss - ff)
        return ((z if zz is None else zz) * SPLIT + xx // 2 * 2 + cc, xx % 2 * SIDE + yy)

    f_plus, f_minus = device(core, s, turn(f + 1)), device(core, s, turn(f - 1))
    s_plus, s_minus = device(core, turn(s + 1), f), device(core, turn(s - 1), f)
    sibling = (z * SPLIT + x // 2 * 2 + 1 - core, t)
    step = 2**level
    partner_z = z + step - 2 * step * (z // step % 2)
    partner = device(core, s, f, partner_z)
    s_peers = [device(core, turn(s + k), f) for k in range(1, SIDE)]
    f_peers = [device(core, s, turn(f + k)) for k in range(1, SIDE)]

    def remote(src, dst, send, recv, to):
        return pltpu.make_async_remote_copy(
            src_ref=src, dst_ref=dst, send_sem=send, recv_sem=recv, device_id=to, device_id_type=MESH
        )

    loads = [
        pltpu.make_async_copy(src.at[0], dst, load_sem.at[i])
        for i, (src, dst) in enumerate(
            ((wd_in, wd), (md_in, md), (wg_in, wg), (wu_in, wu), (mg_in, mg), (mu_in, mu))
        )
    ]
    pieces = depth // CHUNK

    def when(condition, run):
        if isinstance(condition, bool):
            if condition:
                run()
        else:
            pl.when(condition)(run)

    class Wave:
        def __init__(self, w, src, land, col, wide):
            self.w, self.src, self.land, self.col, self.wide = w, src, land, col, wide

        def cols(self, part):
            wide = self.wide
            if part == "all":
                return pl.ds(self.col, wide)
            return pl.ds(self.col + (wide // 2 if part == "high" else 0), wide // 2)

        def block(self, ds, df, part="all"):
            at = core * blocks + turn(s + ds) * SIDE + turn(f + df)
            return self.land.at[at, :, self.cols(part)]

        def group(self, ds, part="all", other=False):
            if other:
                at = (1 - core) * blocks + turn(f + ds) * SIDE
            else:
                at = core * blocks + turn(s + ds) * SIDE
            return self.land.at[pl.ds(at, SIDE), :, self.cols(part)]

        def copy(self, src, dst, slot, to):
            return remote(src, dst, wave_send.at[self.w, slot], wave_recv.at[self.w, slot], to)

        def send(self, src, dst, slot, to):
            self.copy(src, dst, slot, to).start()

        def wait(self, dst, slot):
            self.copy(dst, dst, slot, sibling).wait_recv()

        def own(self):
            return pltpu.make_async_copy(
                self.src.at[:, self.cols("all")], self.block(0, 0), own_sem.at[self.w]
            )

        def start(self):
            to = self.block(0, 0)
            mine = to if self.src is None else self.src.at[:, self.cols("all")]
            self.send(mine, to, 0, f_plus)
            self.send(mine, to, 1, f_minus)
            if self.src is not None:
                self.own().start()

        def near(self):
            self.wait(self.block(0, -1), 0)
            self.wait(self.block(0, 1), 1)
            for df, part, slot, to in ((-1, "low", 2, f_plus), (1, "high", 3, f_minus)):
                ref = self.block(0, df, part)
                self.send(ref, ref, slot, to)

        def far(self):
            self.wait(self.block(0, 2, "low"), 2)
            self.wait(self.block(0, 2, "high"), 3)

        def to_sibling(self, ds, slot):
            ref = self.group(ds)
            self.send(ref, ref, 20 + slot, sibling)

        def spread(self):
            self.far()
            if self.src is not None:
                self.own().wait()
            ref = self.group(0)
            self.send(ref, ref, 4, s_plus)
            self.send(ref, ref, 8, s_minus)
            self.to_sibling(0, 0)

        def onward(self):
            for ds, part, slot, to in ((-1, "low", 4, s_plus), (1, "high", 8, s_minus)):
                self.wait(self.group(ds), slot)
                ref = self.group(ds, part)
                self.send(ref, ref, slot + 8, to)
            self.to_sibling(-1, 1)
            self.to_sibling(1, 2)

        def last(self):
            self.wait(self.group(2, "low"), 12)
            self.wait(self.group(2, "high"), 16)
            self.to_sibling(2, 3)

        def other(self):
            for slot, ds in enumerate((0, -1, 1, 2)):
                self.wait(self.group(ds, other=True), 20 + slot)

        def sent(self):
            for slot in (0, 1):
                self.copy(self.block(0, 0), self.block(0, 0), slot, sibling).wait_send()
            for slot, part in ((2, "low"), (3, "high")):
                self.copy(self.block(0, 0, part), self.block(0, 0, part), slot, sibling).wait_send()
            for slot in (20, 21, 22, 23):
                self.copy(self.group(0), self.group(0), slot, sibling).wait_send()

        def sent_groups(self):
            for slot, part in ((4, "all"), (8, "all"), (12, "low"), (16, "high")):
                self.copy(self.group(0, part), self.group(0, part), slot, sibling).wait_send()

        def spread_block(self, df, src=None):
            ref = self.block(0, df)
            src = ref if src is None else src
            self.send(src, ref, 4 + df % SIDE, s_plus)
            self.send(src, ref, 8 + df % SIDE, s_minus)

        def onward_block(self, df):
            for ds, part, slot, to in ((-1, "low", 4, s_plus), (1, "high", 8, s_minus)):
                self.wait(self.block(ds, df), slot + df % SIDE)
                ref = self.block(ds, df, part)
                self.send(ref, ref, slot + 8 + df % SIDE, to)

        def last_block(self, df):
            self.wait(self.block(2, df, "low"), 12 + df % SIDE)
            self.wait(self.block(2, df, "high"), 16 + df % SIDE)

        def sent_blocks(self):
            for slot, part in ((4, "all"), (8, "all"), (12, "low"), (16, "high")):
                for df in range(SIDE):
                    ref = self.block(0, 0, part)
                    self.copy(ref, ref, slot + df, sibling).wait_send()

    first = Wave(0, x_in, x3, 0, depth)
    peer_g = Wave(1 + pieces, None, gp3, 0, depth)

    def g_wave(i):
        col = i * CHUNK if isinstance(i, int) else at_multiple(i * CHUNK, CHUNK)
        return Wave(1 + i, g_in, g3, col, CHUNK)

    def piece_at(piece):
        return pl.ds(
            piece * CHUNK if isinstance(piece, int) else at_multiple(piece * CHUNK, CHUNK), CHUNK
        )

    def repack(land, flat, start, pairs, cols):
        def body(i, carry):
            b = start + 2 * i
            pair = jnp.concatenate(
                [land[b, :, cols].astype(F32), land[b + 1, :, cols].astype(F32)], 0
            )
            flat[pl.ds(at_multiple(b * rows, 2 * rows), 2 * rows), cols] = pair.astype(BF16)
            return carry

        lax.fori_loop(0, pairs, body, 0)

    def forward(which):
        at = pl.ds(at_multiple(which * half, half), half)
        tokens = xc[at, :]
        g_val = jnp.dot(tokens, wg[...], preferred_element_type=F32)
        gate[at, :] = g_val
        u_val = jnp.dot(tokens, wu[...], preferred_element_type=F32)
        up[at, :] = u_val
        act[at, :] = (g_val * jax.nn.sigmoid(g_val) * u_val).astype(BF16)

    def advance(weight, moment, grad):
        total = MOMENT * moment.astype(F32) + grad
        return (weight.astype(F32) - LEARN * total).astype(BF16)

    weights = ((md, rd, nd_o), (mg, rg, ng_o), (mu, ru, nu_o), (md, rd, nd_o))
    early = EARLY[level]
    rows_early = pl.ds(0, early)
    mine_at = core * blocks + s * SIDE + f
    ahead = [
        remote(src, dst, gossip_send.at[3 * pieces + i], gossip_recv.at[3 * pieces + i], partner)
        for i, (src, dst) in enumerate(
            (
                (g_in, gp3.at[mine_at]),
                (he.at[rows_early], rd.at[rows_early]),
                (actt.at[rows_early], actp.at[rows_early]),
            )
        )
    ]

    def index_of(kind, at):
        if kind == 0:
            return (pl.ds(early, width - early), at)
        return (at, slice(None)) if kind < 3 else (pl.ds(0, early), at)

    def gossip(kind, piece):
        mine, theirs, _ = weights[kind]
        index = index_of(kind, piece_at(piece))
        n = kind * pieces + piece
        return remote(
            mine.at[index], theirs.at[index], gossip_send.at[n], gossip_recv.at[n], partner
        )

    def gossip_start(kind, piece):
        gossip(kind, piece).start()

    def write(kind, piece):
        index = index_of(kind, piece_at(piece))
        _, theirs, to = weights[kind]
        return pltpu.make_async_copy(
            theirs.at[index], to.at[(0, *index)], write_sem.at[kind * pieces + piece]
        )

    def finish(kind, piece):
        index = index_of(kind, piece_at(piece))
        mine, theirs, _ = weights[kind]
        gossip(kind, piece).wait_recv()
        theirs[index] = ((mine[index].astype(F32) + theirs[index].astype(F32)) * 0.5).astype(BF16)
        write(kind, piece).start()

    def repeat(count, run, start=0):
        def body(i, carry):
            run(i)
            return carry

        lax.fori_loop(start, count, body, 0)

    compute = "nocompute" not in FLAGS

    for load in loads:
        load.start()
    barrier = pltpu.get_barrier_semaphore()
    greeted = s_peers + f_peers + [sibling, partner]
    for to in greeted:
        pl.semaphore_signal(barrier, inc=1, device_id=to, device_id_type=MESH)
    pl.semaphore_wait(barrier, len(greeted))

    first.start()
    first.spread_block(0, x_in.at[:, pl.ds(0, depth)])
    ahead[0].start()
    loads[0].wait()
    loads[1].wait()

    def decayed(piece):
        at = piece_at(piece)
        he[rows_early, at] = advance(wd[rows_early, at], md[rows_early, at], 0.0)

    repeat(pieces, decayed)
    ahead[1].start()
    first.near()
    first.spread_block(-1)
    first.spread_block(1)
    first.onward_block(0)
    first.far()
    first.spread_block(2)
    first.own().wait()
    first.to_sibling(0, 0)
    first.onward_block(-1)
    first.onward_block(1)
    repeat(pieces, lambda i: g_wave(i).start())
    first.onward_block(2)
    first.to_sibling(-1, 1)
    first.to_sibling(1, 2)
    repeat(pieces, lambda i: g_wave(i).near())
    repeat(2, lambda i: g_wave(i).spread())

    def token_half(i):
        def own_half():
            for df in (0, -1, 1, 2):
                first.last_block(df)
            first.to_sibling(2, 3)
            loads[2].wait()
            loads[3].wait()
            g_wave(0).onward()

        def other_half():
            first.other()
            g_wave(0).last()
            g_wave(1).onward()

        when(i == 0, own_half)
        when(i == 1, other_half)
        which = core + i * (1 - 2 * core)
        if compute:
            repack(x3, xc, which * blocks, blocks // 2, pl.ds(0, depth))
            forward(which)
        when(i == 0, lambda: g_wave(2).spread())
        when(i == 1, lambda: g_wave(3).spread())

    repeat(2, token_half)
    if compute:
        actt[...] = act[...].T
    ahead[2].start()

    def down(w):
        g_wave(w).other()
        at = piece_at(w)
        if compute:
            repack(g3, gc, 0, blocks, at)
            grad = jnp.dot(actt[...], gc[:, at], preferred_element_type=F32)
            md[:, at] = advance(wd[:, at], md[:, at], grad)
        gossip_start(0, w)
        when(w + 1 < pieces, lambda: g_wave(w + 1).last())
        when(w + 2 < pieces, lambda: g_wave(w + 2).onward())
        when(w + 4 < pieces, lambda: g_wave(w + 4).spread())

    repeat(pieces, down)

    def backward(which):
        at = pl.ds(at_multiple(which * half, half), half)
        act_grad = lax.dot_general(
            gc[at, :], wd[...], (((1,), (1,)), ((), ())), preferred_element_type=F32
        )
        g_val, u_val = gate[at, :], up[at, :]
        sig = jax.nn.sigmoid(g_val)
        gb[at, :] = (act_grad * u_val * sig * (1.0 + g_val * (1.0 - sig))).astype(BF16)
        ub[at, :] = (act_grad * (g_val * sig)).astype(BF16)

    ahead[0].wait_recv()
    peer_g.start()
    if compute:
        repeat(2, backward)
    peer_g.near()
    loads[4].wait()
    loads[5].wait()

    def columns(piece):
        at = piece_at(piece)
        if compute:
            turned = xc[:, at].T
            mg[at, :] = advance(
                wg[at, :], mg[at, :], jnp.dot(turned, gb[...], preferred_element_type=F32)
            )
        gossip_start(1, piece)
        if compute:
            mu[at, :] = advance(
                wu[at, :], mu[at, :], jnp.dot(turned, ub[...], preferred_element_type=F32)
            )
        gossip_start(2, piece)

    repeat(pieces, columns)

    first.sent()
    first.sent_blocks()

    def g_sent(i):
        g_wave(i).sent()
        g_wave(i).sent_groups()

    repeat(pieces, g_sent)

    def partial(kind, which, at):
        part = pl.ds(at_multiple(which * half, half), half)
        if kind == 0:
            return jnp.dot(act[part, :], wd[:, at], preferred_element_type=F32)
        nt = (((1,), (1,)), ((), ()))
        return lax.dot_general(
            gb[part, :], wg[at, :], nt, preferred_element_type=F32
        ) + lax.dot_general(ub[part, :], wu[at, :], nt, preferred_element_type=F32)

    sums = ((x3, sx, px, out_o), (g3, sg, pg, gin_o))

    def pair_copy(kind, piece):
        stage, theirs, _, _ = sums[kind]
        at = piece_at(piece)
        return remote(
            stage.at[pl.ds((1 - core) * blocks, blocks), :, at],
            theirs.at[:, :, at],
            pair_send.at[kind, piece],
            pair_recv.at[kind, piece],
            sibling,
        )

    def s_copy(kind, k):
        stage, _, theirs, _ = sums[kind]
        return remote(
            stage.at[pl.ds(core * blocks + turn(s + k) * SIDE, SIDE)],
            theirs.at[pl.ds(k * SIDE, SIDE)],
            sum_send.at[kind, k],
            sum_recv.at[kind, k],
            s_peers[k - 1],
        )

    def f_copy(kind, k):
        stage, _, theirs, _ = sums[kind]
        return remote(
            stage.at[core * blocks + s * SIDE + turn(f + k)],
            theirs.at[k],
            sum_send.at[kind, SIDE + k],
            sum_recv.at[kind, SIDE + k],
            f_peers[k - 1],
        )

    def for_sibling(kind, piece):
        stage = sums[kind][0]
        at = piece_at(piece)
        value = partial(kind, 1 - core, at)
        for i in range(blocks):
            stage[(1 - core) * blocks + i, :, at] = value[i * rows : (i + 1) * rows].astype(BF16)
        pair_copy(kind, piece).start()

    def with_sibling(kind, piece):
        stage, theirs, _, _ = sums[kind]
        at = piece_at(piece)
        value = partial(kind, core, at)
        pair_copy(kind, piece).wait_recv()
        for i in range(blocks):
            stage[core * blocks + i, :, at] = (
                value[i * rows : (i + 1) * rows] + theirs[i, :, at].astype(F32)
            ).astype(BF16)

    def along_s(kind):
        stage, _, theirs, _ = sums[kind]
        for k in range(1, SIDE):
            s_copy(kind, k).wait_recv()

        def add(i):
            b = core * blocks + s * SIDE + i
            value = stage[b].astype(F32)
            for k in range(1, SIDE):
                value = value + theirs[k * SIDE + i].astype(F32)
            stage[b] = value.astype(BF16)

        repeat(SIDE, add)
        for k in range(1, SIDE):
            f_copy(kind, k).start()

    def total(kind):
        stage, _, theirs, to = sums[kind]
        for k in range(1, SIDE):
            f_copy(kind, k).wait_recv()
        value = stage[mine_at].astype(F32)
        for k in range(1, SIDE):
            value = value + theirs[k].astype(F32)
        to[...] = value

    peer_g.spread()
    repeat(pieces, functools.partial(for_sibling, 0))
    peer_g.onward()
    repeat(pieces, functools.partial(for_sibling, 1))
    peer_g.last()
    for kind in (0, 1):
        repeat(pieces, functools.partial(with_sibling, kind))
        for k in range(1, SIDE):
            s_copy(kind, k).start()

    peer_g.other()
    repack(gp3, gc, 0, blocks, pl.ds(0, depth))
    ahead[1].wait_recv()
    ahead[2].wait_recv()

    def peer_rows(piece):
        at = piece_at(piece)
        grad = jnp.dot(actp[rows_early, :], gc[:, at], preferred_element_type=F32)
        theirs = (rd[rows_early, at].astype(F32) - LEARN * grad).astype(BF16)
        both = md[rows_early, at].astype(F32) + theirs.astype(F32)
        rd[rows_early, at] = (both * 0.5).astype(BF16)
        write(3, piece).start()

    repeat(pieces, peer_rows)
    for kind in (0, 1):
        along_s(kind)

    repeat(pieces, functools.partial(finish, 0))

    def finish_both(piece):
        finish(1, piece)
        finish(2, piece)

    repeat(pieces - 3, finish_both)
    for kind in (0, 1):
        total(kind)
    repeat(pieces, finish_both, pieces - 3)

    peer_g.sent()
    peer_g.sent_groups()
    for kind in (0, 1):
        repeat(pieces, lambda piece: pair_copy(kind, piece).wait_send())
        for k in range(1, SIDE):
            s_copy(kind, k).wait_send()
            f_copy(kind, k).wait_send()
    for copy in ahead:
        copy.wait_send()
    for kind in range(4):
        if kind < 3:
            repeat(pieces, lambda piece: gossip(kind, piece).wait_send())
        repeat(pieces, lambda piece: write(kind, piece).wait())


def call(level, *args):
    x_in, _, wg, _, wd = args[:5]
    rows, depth = x_in.shape
    width = wg.shape[2]
    blocks = SIDE * SIDE
    tokens = 2 * blocks * rows
    pieces = depth // CHUNK
    any_space = pl.BlockSpec(memory_space=pl.ANY)
    vmem = pl.BlockSpec(memory_space=pltpu.VMEM)
    dma = pltpu.SemaphoreType.DMA
    tall, flat = pltpu.VMEM((depth, width), BF16), pltpu.VMEM((width, depth), BF16)
    return pl.pallas_call(
        functools.partial(kernel, level),
        name="step_level_" + str(level),
        out_shape=(
            jax.ShapeDtypeStruct((rows, depth), F32),
            jax.ShapeDtypeStruct((rows, depth), F32),
            jax.ShapeDtypeStruct(wg.shape, BF16),
            jax.ShapeDtypeStruct(wg.shape, BF16),
            jax.ShapeDtypeStruct(wd.shape, BF16),
        ),
        in_specs=[any_space] * 8,
        out_specs=(vmem, vmem, any_space, any_space, any_space),
        scratch_shapes=[
            pltpu.VMEM((2 * blocks, rows, depth), BF16),
            pltpu.VMEM((2 * blocks, rows, depth), BF16),
            pltpu.VMEM((tokens, depth), BF16),
            pltpu.VMEM((tokens, depth), BF16),
            tall,
            tall,
            flat,
            tall,
            tall,
            flat,
            tall,
            tall,
            flat,
            pltpu.VMEM((tokens, width), F32),
            pltpu.VMEM((tokens, width), F32),
            pltpu.VMEM((tokens, width), BF16),
            pltpu.VMEM((tokens, width), BF16),
            pltpu.VMEM((tokens, width), BF16),
            pltpu.VMEM((width, tokens), BF16),
            pltpu.VMEM((max(EARLY), depth), BF16),
            pltpu.VMEM((2 * blocks, rows, depth), BF16),
            pltpu.VMEM((max(EARLY), tokens), BF16),
            pltpu.VMEM((blocks, rows, depth), BF16),
            pltpu.VMEM((blocks, rows, depth), BF16),
            pltpu.VMEM((blocks, rows, depth), BF16),
            pltpu.VMEM((blocks, rows, depth), BF16),
            dma((6,)),
            dma((1 + pieces,)),
            dma((2 + pieces, 24)),
            dma((2 + pieces, 24)),
            dma((2, pieces)),
            dma((2, pieces)),
            dma((2, 2 * SIDE)),
            dma((2, 2 * SIDE)),
            dma((3 * pieces + 3,)),
            dma((3 * pieces + 3,)),
            dma((4 * pieces,)),
        ],
        compiler_params=pltpu.CompilerParams(
            collective_id=level, has_side_effects=True, vmem_limit_bytes=60 << 20
        ),
    )(*args)


def per_device(*args):
    *arrays, step_count = args
    levels = (lax.axis_size("rep") // SPLIT).bit_length() - 1
    out, back, *weights = lax.switch(
        jnp.mod(step_count, levels),
        [functools.partial(call, level) for level in range(levels)],
        *arrays,
    )
    block_out = (arrays[0].astype(F32) + out).astype(BF16)
    input_grad = (arrays[1].astype(F32) + back).astype(BF16)
    return (block_out, input_grad, *weights)


def solution(mesh):
    rows, columns, across = P(("rep", "tp"), None), P("rep", None, "tp"), P("rep", "tp", None)
    return jax.shard_map(
        per_device,
        mesh=mesh,
        in_specs=(rows, rows, columns, columns, across, columns, columns, across, P()),
        out_specs=(rows, rows, columns, columns, across),
        check_vma=False,
    )
```

profile of v0, /device:TPU:1, one launch (start us, length us, event | category | flops | bytes accessed | tf_op | source)
XLA Modules:
  0.0 205.1 jit_solution(5495729459017069630)
XLA Ops:
  1.3 198.2 %conditional.1 = ((f32[24,2560]{1,0:T(8,128)S(1)}, f32[24,2560]{1,0:T(8,128)S(1)}, bf16[1,2560,256]{2,1,0:T(8,128)(2,1)S(1)}, bf16[1,2560,256]{2,1,0:T(8,128)(2,1)S(1)}, bf16[1,256,2560]{2,1,0:T(8,128)(2,1)})) conditional(s32[]{:T(128)} %clamp.3, (bf16[24,2560]{1,0:T(8,128)(2,1)}, bf16[24,2560]{1,0:T(8,128)(2,1)}, ...), branch_computations={%region_0.1_spmd, %region_1.2_spmd, %region_2.3_spmd} | conditional | bytes 8 | solution.py:665
  1.7 197.5 %step_level_2.1 = (f32[24,2560]{1,0:T(8,128)S(1)}, f32[24,2560]{1,0:T(8,128)S(1)}, bf16[1,2560,256]{2,1,0:T(8,128)(2,1)S(1)}, bf16[1,2560,256]{2,1,0:T(8,128)(2,1)S(1)}, bf16[1,256,2560]{2,1,0:T(8,128)(2,1)}) custom-call(bf16[24,2560]{1,0:T(8,128)(2,1)} %get-tuple-element.64.x_in, bf16[24,2560]{1,0:T(8,128)(2,1)} %get-tuple-element.65.g_in, ...), custom_call_target="tpu_custom_call" | custom-call | tf_op jit(solution)/shard_map/cond/branch_2_fun/step_level_2/pallas_call | solution.py:605
  199.5 1.7 add_convert_fusion
  201.2 1.1 copy.33
  202.2 0.0 copy-start
  202.2 1.1 copy.34
  203.3 0.7 copy-done
  204.0 1.1 copy.35
Async XLA Ops:
  202.2 1.8 copy-start
where the time goes:
time: 206 us; the launch traced here: 205 us
  Pallas kernels  197 us (96%)
  local copies, waits for them, and re-layouts  3.9 us (2%)
    pallas_call x1, Pallas kernels, call(): pl.pallas_call(functools.partial(kernel, level), name='step_level_' + str...  197 us

commit v1 on v0

--- a/solution.py
+++ b/solution.py
@@ -13,8 +13,7 @@
 MOMENT = 0.9
 LEARN = 0.001
 CHUNK = 512
-FLAGS = ()
-EARLY = (192, 80, 80)
+EARLY = (192, 96, 96)
 F32 = jnp.float32
 BF16 = jnp.bfloat16
 
@@ -64,6 +63,8 @@
     sg,
     px,
     pg,
+    xo,
+    go,
     load_sem,
     own_sem,
     wave_send,
@@ -74,7 +75,6 @@
     sum_recv,
     gossip_send,
     gossip_recv,
-    write_sem,
 ):
     rows, depth = x_in.shape
     width = wg.shape[1]
@@ -114,6 +114,10 @@
             ((wd_in, wd), (md_in, md), (wg_in, wg), (wu_in, wu), (mg_in, mg), (mu_in, mu))
         )
     ]
+    loads += [
+        pltpu.make_async_copy(src, dst, load_sem.at[6 + i])
+        for i, (src, dst) in enumerate(((x_in, xo), (g_in, go)))
+    ]
     pieces = depth // CHUNK
 
     def when(condition, run):
@@ -219,6 +223,33 @@
             for slot, part in ((4, "all"), (8, "all"), (12, "low"), (16, "high")):
                 self.copy(self.group(0, part), self.group(0, part), slot, sibling).wait_send()
 
+        def step(self, n):
+            if n == 0:
+                self.start()
+                self.spread_block(0, self.src.at[:, self.cols("all")])
+            elif n == 1:
+                self.near()
+                self.spread_block(-1)
+                self.spread_block(1)
+                self.onward_block(0)
+            elif n == 2:
+                self.far()
+                self.spread_block(2)
+                self.own().wait()
+                self.to_sibling(0, 0)
+                self.onward_block(-1)
+                self.onward_block(1)
+            elif n == 3:
+                self.onward_block(2)
+                self.to_sibling(-1, 1)
+                self.to_sibling(1, 2)
+            elif n == 4:
+                for df in (0, -1, 1, 2):
+                    self.last_block(df)
+                self.to_sibling(2, 3)
+            else:
+                self.other()
+
         def spread_block(self, df, src=None):
             ref = self.block(0, df)
             src = ref if src is None else src
@@ -242,11 +273,8 @@
                     self.copy(ref, ref, slot + df, sibling).wait_send()
 
     first = Wave(0, x_in, x3, 0, depth)
-    peer_g = Wave(1 + pieces, None, gp3, 0, depth)
-
-    def g_wave(i):
-        col = i * CHUNK if isinstance(i, int) else at_multiple(i * CHUNK, CHUNK)
-        return Wave(1 + i, g_in, g3, col, CHUNK)
+    g_waves = [Wave(1 + i, g_in, g3, i * depth // 2, depth // 2) for i in (0, 1)]
+    peer_g = Wave(3, None, gp3, 0, depth)
 
     def piece_at(piece):
         return pl.ds(
@@ -277,7 +305,7 @@
         total = MOMENT * moment.astype(F32) + grad
         return (weight.astype(F32) - LEARN * total).astype(BF16)
 
-    weights = ((md, rd, nd_o), (mg, rg, ng_o), (mu, ru, nu_o), (md, rd, nd_o))
+    weights = ((md, rd, nd_o), (mg, rg, ng_o), (mu, ru, nu_o))
     early = EARLY[level]
     rows_early = pl.ds(0, early)
     mine_at = core * blocks + s * SIDE + f
@@ -295,7 +323,7 @@
     def index_of(kind, at):
         if kind == 0:
             return (pl.ds(early, width - early), at)
-        return (at, slice(None)) if kind < 3 else (pl.ds(0, early), at)
+        return (at, slice(None))
 
     def gossip(kind, piece):
         mine, theirs, _ = weights[kind]
@@ -308,19 +336,12 @@
     def gossip_start(kind, piece):
         gossip(kind, piece).start()
 
-    def write(kind, piece):
-        index = index_of(kind, piece_at(piece))
-        _, theirs, to = weights[kind]
-        return pltpu.make_async_copy(
-            theirs.at[index], to.at[(0, *index)], write_sem.at[kind * pieces + piece]
-        )
-
     def finish(kind, piece):
         index = index_of(kind, piece_at(piece))
-        mine, theirs, _ = weights[kind]
+        mine, theirs, to = weights[kind]
         gossip(kind, piece).wait_recv()
-        theirs[index] = ((mine[index].astype(F32) + theirs[index].astype(F32)) * 0.5).astype(BF16)
-        write(kind, piece).start()
+        both = mine[index].astype(F32) + theirs[index].astype(F32)
+        to[(0, *index)] = (both * 0.5).astype(BF16)
 
     def repeat(count, run, start=0):
         def body(i, carry):
@@ -328,130 +349,6 @@
             return carry
 
         lax.fori_loop(start, count, body, 0)
-
-    compute = "nocompute" not in FLAGS
-
-    for load in loads:
-        load.start()
-    barrier = pltpu.get_barrier_semaphore()
-    greeted = s_peers + f_peers + [sibling, partner]
-    for to in greeted:
-        pl.semaphore_signal(barrier, inc=1, device_id=to, device_id_type=MESH)
-    pl.semaphore_wait(barrier, len(greeted))
-
-    first.start()
-    first.spread_block(0, x_in.at[:, pl.ds(0, depth)])
-    ahead[0].start()
-    loads[0].wait()
-    loads[1].wait()
-
-    def decayed(piece):
-        at = piece_at(piece)
-        he[rows_early, at] = advance(wd[rows_early, at], md[rows_early, at], 0.0)
-
-    repeat(pieces, decayed)
-    ahead[1].start()
-    first.near()
-    first.spread_block(-1)
-    first.spread_block(1)
-    first.onward_block(0)
-    first.far()
-    first.spread_block(2)
-    first.own().wait()
-    first.to_sibling(0, 0)
-    first.onward_block(-1)
-    first.onward_block(1)
-    repeat(pieces, lambda i: g_wave(i).start())
-    first.onward_block(2)
-    first.to_sibling(-1, 1)
-    first.to_sibling(1, 2)
-    repeat(pieces, lambda i: g_wave(i).near())
-    repeat(2, lambda i: g_wave(i).spread())
-
-    def token_half(i):
-        def own_half():
-            for df in (0, -1, 1, 2):
-                first.last_block(df)
-            first.to_sibling(2, 3)
-            loads[2].wait()
-            loads[3].wait()
-            g_wave(0).onward()
-
-        def other_half():
-            first.other()
-            g_wave(0).last()
-            g_wave(1).onward()
-
-        when(i == 0, own_half)
-        when(i == 1, other_half)
-        which = core + i * (1 - 2 * core)
-        if compute:
-            repack(x3, xc, which * blocks, blocks // 2, pl.ds(0, depth))
-            forward(which)
-        when(i == 0, lambda: g_wave(2).spread())
-        when(i == 1, lambda: g_wave(3).spread())
-
-    repeat(2, token_half)
-    if compute:
-        actt[...] = act[...].T
-    ahead[2].start()
-
-    def down(w):
-        g_wave(w).other()
-        at = piece_at(w)
-        if compute:
-            repack(g3, gc, 0, blocks, at)
-            grad = jnp.dot(actt[...], gc[:, at], preferred_element_type=F32)
-            md[:, at] = advance(wd[:, at], md[:, at], grad)
-        gossip_start(0, w)
-        when(w + 1 < pieces, lambda: g_wave(w + 1).last())
-        when(w + 2 < pieces, lambda: g_wave(w + 2).onward())
-        when(w + 4 < pieces, lambda: g_wave(w + 4).spread())
-
-    repeat(pieces, down)
-
-    def backward(which):
-        at = pl.ds(at_multiple(which * half, half), half)
-        act_grad = lax.dot_general(
-            gc[at, :], wd[...], (((1,), (1,)), ((), ())), preferred_element_type=F32
-        )
-        g_val, u_val = gate[at, :], up[at, :]
-        sig = jax.nn.sigmoid(g_val)
-        gb[at, :] = (act_grad * u_val * sig * (1.0 + g_val * (1.0 - sig))).astype(BF16)
-        ub[at, :] = (act_grad * (g_val * sig)).astype(BF16)
-
-    ahead[0].wait_recv()
-    peer_g.start()
-    if compute:
-        repeat(2, backward)
-    peer_g.near()
-    loads[4].wait()
-    loads[5].wait()
-
-    def columns(piece):
-        at = piece_at(piece)
-        if compute:
-            turned = xc[:, at].T
-            mg[at, :] = advance(
-                wg[at, :], mg[at, :], jnp.dot(turned, gb[...], preferred_element_type=F32)
-            )
-        gossip_start(1, piece)
-        if compute:
-            mu[at, :] = advance(
-                wu[at, :], mu[at, :], jnp.dot(turned, ub[...], preferred_element_type=F32)
-            )
-        gossip_start(2, piece)
-
-    repeat(pieces, columns)
-
-    first.sent()
-    first.sent_blocks()
-
-    def g_sent(i):
-        g_wave(i).sent()
-        g_wave(i).sent_groups()
-
-    repeat(pieces, g_sent)
 
     def partial(kind, which, at):
         part = pl.ds(at_multiple(which * half, half), half)
@@ -463,6 +360,7 @@
         ) + lax.dot_general(ub[part, :], wu[at, :], nt, preferred_element_type=F32)
 
     sums = ((x3, sx, px, out_o), (g3, sg, pg, gin_o))
+    given = (xo, go)
 
     def pair_copy(kind, piece):
         stage, theirs, _, _ = sums[kind]
@@ -536,17 +434,122 @@
         value = stage[mine_at].astype(F32)
         for k in range(1, SIDE):
             value = value + theirs[k].astype(F32)
-        to[...] = value
-
+        loads[6 + kind].wait()
+        to[...] = (given[kind][...].astype(F32) + value).astype(BF16)
+
+    for load in loads:
+        load.start()
+    barrier = pltpu.get_barrier_semaphore()
+    greeted = s_peers + f_peers + [sibling, partner]
+    for to in greeted:
+        pl.semaphore_signal(barrier, inc=1, device_id=to, device_id_type=MESH)
+    pl.semaphore_wait(barrier, len(greeted))
+
+    first.step(0)
+    ahead[0].start()
+    loads[0].wait()
+    loads[1].wait()
+
+    def decayed(piece):
+        at = piece_at(piece)
+        he[rows_early, at] = advance(wd[rows_early, at], md[rows_early, at], 0.0)
+
+    repeat(pieces, decayed)
+    ahead[1].start()
+    first.step(1)
+    first.step(2)
+    g_waves[0].step(0)
+    first.step(3)
+    g_waves[0].step(1)
+    g_waves[1].step(0)
+
+    def token_half(i):
+        def own_half():
+            first.step(4)
+            loads[2].wait()
+            loads[3].wait()
+
+        def other_half():
+            g_waves[0].step(2)
+            g_waves[1].step(1)
+            first.step(5)
+
+        when(i == 0, own_half)
+        when(i == 1, other_half)
+        which = core + i * (1 - 2 * core)
+        repack(x3, xc, which * blocks, blocks // 2, pl.ds(0, depth))
+        forward(which)
+
+    repeat(2, token_half)
+    g_waves[0].step(3)
+    g_waves[1].step(2)
+    actt[...] = act[...].T
+    ahead[2].start()
+    g_waves[0].step(4)
+    g_waves[1].step(3)
+
+    def down(piece):
+        at = piece_at(piece)
+        grad = jnp.dot(actt[...], gc[:, at], preferred_element_type=F32)
+        md[:, at] = advance(wd[:, at], md[:, at], grad)
+        gossip(0, piece).start()
+
+    g_waves[0].step(5)
+    repack(g3, gc, 0, blocks, pl.ds(0, depth // 2))
+    repeat(pieces // 2, down)
+    first.sent()
+    first.sent_blocks()
+    g_waves[1].step(4)
+    repeat(pieces, functools.partial(for_sibling, 0))
+    g_waves[1].step(5)
+    repack(g3, gc, 0, blocks, pl.ds(depth // 2, depth // 2))
+    repeat(pieces, down, pieces // 2)
+    ahead[0].wait_recv()
+    peer_g.start()
+    repeat(pieces, functools.partial(with_sibling, 0))
+    for k in range(1, SIDE):
+        s_copy(0, k).start()
+
+    def backward(which):
+        at = pl.ds(at_multiple(which * half, half), half)
+        act_grad = lax.dot_general(
+            gc[at, :], wd[...], (((1,), (1,)), ((), ())), preferred_element_type=F32
+        )
+        g_val, u_val = gate[at, :], up[at, :]
+        sig = jax.nn.sigmoid(g_val)
+        gb[at, :] = (act_grad * u_val * sig * (1.0 + g_val * (1.0 - sig))).astype(BF16)
+        ub[at, :] = (act_grad * (g_val * sig)).astype(BF16)
+
+    repeat(2, backward)
+    peer_g.near()
+    loads[4].wait()
+    loads[5].wait()
+
+    def columns(piece):
+        at = piece_at(piece)
+        turned = xc[:, at].T
+        mg[at, :] = advance(
+            wg[at, :], mg[at, :], jnp.dot(turned, gb[...], preferred_element_type=F32)
+        )
+        gossip(1, piece).start()
+        mu[at, :] = advance(
+            wu[at, :], mu[at, :], jnp.dot(turned, ub[...], preferred_element_type=F32)
+        )
+        gossip(2, piece).start()
+
+    repeat(pieces, columns)
     peer_g.spread()
-    repeat(pieces, functools.partial(for_sibling, 0))
+
+    for one in g_waves:
+        one.sent()
+        one.sent_blocks()
+    repeat(pieces, functools.partial(for_sibling, 1))
     peer_g.onward()
-    repeat(pieces, functools.partial(for_sibling, 1))
+    repeat(pieces, functools.partial(with_sibling, 1))
+    for k in range(1, SIDE):
+        s_copy(1, k).start()
     peer_g.last()
-    for kind in (0, 1):
-        repeat(pieces, functools.partial(with_sibling, kind))
-        for k in range(1, SIDE):
-            s_copy(kind, k).start()
+    along_s(0)
 
     peer_g.other()
     repack(gp3, gc, 0, blocks, pl.ds(0, depth))
@@ -558,12 +561,10 @@
         grad = jnp.dot(actp[rows_early, :], gc[:, at], preferred_element_type=F32)
         theirs = (rd[rows_early, at].astype(F32) - LEARN * grad).astype(BF16)
         both = md[rows_early, at].astype(F32) + theirs.astype(F32)
-        rd[rows_early, at] = (both * 0.5).astype(BF16)
-        write(3, piece).start()
+        nd_o[0, rows_early, at] = (both * 0.5).astype(BF16)
 
     repeat(pieces, peer_rows)
-    for kind in (0, 1):
-        along_s(kind)
+    along_s(1)
 
     repeat(pieces, functools.partial(finish, 0))
 
@@ -585,10 +586,8 @@
             f_copy(kind, k).wait_send()
     for copy in ahead:
         copy.wait_send()
-    for kind in range(4):
-        if kind < 3:
-            repeat(pieces, lambda piece: gossip(kind, piece).wait_send())
-        repeat(pieces, lambda piece: write(kind, piece).wait())
+    for kind in range(3):
+        repeat(pieces, lambda piece: gossip(kind, piece).wait_send())
 
 
 def call(level, *args):
@@ -606,14 +605,14 @@
         functools.partial(kernel, level),
         name="step_level_" + str(level),
         out_shape=(
-            jax.ShapeDtypeStruct((rows, depth), F32),
-            jax.ShapeDtypeStruct((rows, depth), F32),
+            jax.ShapeDtypeStruct((rows, depth), BF16),
+            jax.ShapeDtypeStruct((rows, depth), BF16),
             jax.ShapeDtypeStruct(wg.shape, BF16),
             jax.ShapeDtypeStruct(wg.shape, BF16),
             jax.ShapeDtypeStruct(wd.shape, BF16),
         ),
         in_specs=[any_space] * 8,
-        out_specs=(vmem, vmem, any_space, any_space, any_space),
+        out_specs=(vmem,) * 5,
         scratch_shapes=[
             pltpu.VMEM((2 * blocks, rows, depth), BF16),
             pltpu.VMEM((2 * blocks, rows, depth), BF16),
@@ -641,35 +640,57 @@
             pltpu.VMEM((blocks, rows, depth), BF16),
             pltpu.VMEM((blocks, rows, depth), BF16),
             pltpu.VMEM((blocks, rows, depth), BF16),
-            dma((6,)),
-            dma((1 + pieces,)),
-            dma((2 + pieces, 24)),
-            dma((2 + pieces, 24)),
+            pltpu.VMEM((rows, depth), BF16),
+            pltpu.VMEM((rows, depth), BF16),
+            dma((8,)),
+            dma((3,)),
+            dma((4, 24)),
+            dma((4, 24)),
             dma((2, pieces)),
             dma((2, pieces)),
             dma((2, 2 * SIDE)),
             dma((2, 2 * SIDE)),
             dma((3 * pieces + 3,)),
             dma((3 * pieces + 3,)),
-            dma((4 * pieces,)),
         ],
         compiler_params=pltpu.CompilerParams(
-            collective_id=level, has_side_effects=True, vmem_limit_bytes=60 << 20
+            collective_id=level, has_side_effects=True, vmem_limit_bytes=57 << 20
         ),
     )(*args)
+
+
+def store_kernel(*refs):
+    count = len(refs) // 2
+    sem = refs[-1]
+    copies = [
+        pltpu.make_async_copy(refs[i], refs[count + i], sem.at[i]) for i in range(count)
+    ]
+    for copy in copies:
+        copy.start()
+    for copy in copies:
+        copy.wait()
+
+
+def store(*arrays):
+    return pl.pallas_call(
+        store_kernel,
+        name="store",
+        out_shape=tuple(jax.ShapeDtypeStruct(a.shape, a.dtype) for a in arrays),
+        in_specs=[pl.BlockSpec(memory_space=pltpu.VMEM)] * len(arrays),
+        out_specs=(pl.BlockSpec(memory_space=pl.ANY),) * len(arrays),
+        scratch_shapes=[pltpu.SemaphoreType.DMA((len(arrays),))],
+    )(*arrays)
 
 
 def per_device(*args):
     *arrays, step_count = args
     levels = (lax.axis_size("rep") // SPLIT).bit_length() - 1
-    out, back, *weights = lax.switch(
+    results = lax.switch(
         jnp.mod(step_count, levels),
         [functools.partial(call, level) for level in range(levels)],
         *arrays,
     )
-    block_out = (arrays[0].astype(F32) + out).astype(BF16)
-    input_grad = (arrays[1].astype(F32) + back).astype(BF16)
-    return (block_out, input_grad, *weights)
+    return store(*results)
 
 
 def solution(mesh):

time: 206 us -> 112 us (0.54)
  Pallas kernels: 197 us -> 110 us
  local copies, waits for them, and re-layouts: 3.9 us -> 0 us
    pallas_call x1, Pallas kernels: 197 us -> 107 us  [call(): pl.pallas_call(functools.partial(kernel, level), name='step_level_' + str...]
    unnamed x5 -> x0, local copies, waits for them, and re-layouts: 3.9 us -> none
    pallas_call x0 -> x1, Pallas kernels: none -> 3.36 us  [store(): pl.pallas_call(store_kernel, name='store', out_shape=tuple((jax.ShapeDtyp...]
where the time goes in v1:
time: 112 us
  Pallas kernels  110 us (98%)
  between operations  1.5 us (1%)
    pallas_call x1, Pallas kernels, call(): pl.pallas_call(functools.partial(kernel, level), name='step_level_' + str...  107 us
    pallas_call x1, Pallas kernels, store(): pl.pallas_call(store_kernel, name='store', out_shape=tuple((jax.ShapeDtyp...  3.36 us

profile of v1, /device:TPU:1, one launch (start us, length us, event | category | flops | bytes accessed | tf_op | source)
XLA Modules:
  0.0 112.0 jit_solution(100120981513947656)
XLA Ops:
  1.3 107.1 %conditional.1 = ((bf16[24,2560]{1,0:T(8,128)(2,1)S(1)}, bf16[24,2560]{1,0:T(8,128)(2,1)S(1)}, bf16[1,2560,256]{2,1,0:T(8,128)(2,1)S(1)}, bf16[1,2560,256]{2,1,0:T(8,128)(2,1)S(1)}, bf16[1,256,2560]{2,1,0:T(8,128)(2,1)})) conditional(s32[]{:T(128)} %clamp.3, (bf16[24,2560]{1,0:T(8,128)(2,1)}, bf16[24,2560]{1,0:T(8,128)(2,1)}, ...), branch_computations={%region_0.1_spmd, %region_1.2_spmd, %region_2.3_spmd} | conditional | bytes 8 | solution.py:688
  1.3 106.8 %step_level_0.1 = (bf16[24,2560]{1,0:T(8,128)(2,1)S(1)}, bf16[24,2560]{1,0:T(8,128)(2,1)S(1)}, bf16[1,2560,256]{2,1,0:T(8,128)(2,1)S(1)}, bf16[1,2560,256]{2,1,0:T(8,128)(2,1)S(1)}, bf16[1,256,2560]{2,1,0:T(8,128)(2,1)}) custom-call(bf16[24,2560]{1,0:T(8,128)(2,1)} %get-tuple-element.48.x_in, bf16[24,2560]{1,0:T(8,128)(2,1)} %get-tuple-element.49.g_in, ...), custom_call_target="tpu_custom_call" | custom-call | tf_op jit(solution)/shard_map/cond/branch_0_fun/step_level_0/pallas_call | solution.py:604
  108.4 3.4 %store.1 = (bf16[24,2560]{1,0:T(8,128)(2,1)}, bf16[24,2560]{1,0:T(8,128)(2,1)}, bf16[1,2560,256]{2,1,0:T(8,128)(2,1)}, bf16[1,2560,256]{2,1,0:T(8,128)(2,1)}, bf16[1,256,2560]{2,1,0:T(8,128)(2,1)}) custom-call(bf16[24,2560]{1,0:T(8,128)(2,1)S(1)} %get-tuple-element.82.refs_0_, bf16[24,2560]{1,0:T(8,128)(2,1)S(1)} %get-tuple-element.83.refs_1_, ...), custom_call_target="tpu_custom_call" | custom-call | tf_op jit(solution)/shard_map/store/pallas_call | solution.py:675
